TPU v7x, 32 devices: a whole 2x2x4 slice. The times are simulated.
32 devices in a mesh: groups: 2 (over x), blk: 16 (over z, y, core).
Axes of the slice: x: 2, y: 2, z: 4, core: 2. Of those that a mesh axis runs over, the one named last changes fastest.
Arguments:
- queries: bfloat16 [12288, 3072], P(('groups', 'blk')), parts along dimension 0, may hold values from -4.5 to 4.5
- keys_values: bfloat16 [2, 12288, 3072], P(None, ('groups', 'blk')), parts along dimension 1, may hold values from -4.5 to 4.5
- key_blocks: int32 [96, 8], P(('groups', 'blk')), parts along dimension 0, may hold values from 0 to 47, as said below
- pair_count: int32 [96], P(('groups', 'blk')), parts along dimension 0, may hold values from 6 to 8
Outputs:
- attended: bfloat16 [12288, 3072], P(('groups', 'blk')), parts along dimension 0
There are 2 independent parts, one for each index of `groups`. A program takes and returns all parts, laid end to end along the dimension named above; each array names one. Nothing has to cross between parts.
Inputs may be any that keep to these rules, and one draw needn't show every extreme that they name: `key_blocks`: row r holds 8 distinct blocks, all held by devices at most 2 places away from the device of block r along the closed cycle of devices (block b lies on device b // 3, devices 0 and the last are neighbours); the first entry is r itself. Entries at j >= pair_count[r] are not pairs.
All inputs are finite; a program needn't handle non-finite values.
Results may differ from a plain program's by a relative error of at most 0.0046.
Values may be sent and summed in bfloat16 or wider, within the bound.
A program may use at most 128 MiB of HBM per device.

v0:
```python
import jax
import jax.numpy as jnp
from jax import lax
from jax.sharding import PartitionSpec as P

H = 24
HD = 128
BLK = 128
REACH = 2
NB = 8


def passed_along(value, axis, steps):
    count = lax.axis_size(axis)
    pairs = [(source, (source + steps) % count) for source in range(count)]
    return lax.ppermute(value, axis, pairs)


def attend(qblock, key_rows, value_rows, live_mask):
    scores = jnp.einsum(
        "qhd,khd->hqk", qblock, key_rows, preferred_element_type=jnp.float32
    ) * HD ** (-0.5)
    scores = jnp.where(live_mask[None, None, :], scores, -1e30)
    row_max = jnp.max(scores, axis=-1, keepdims=True)
    weights = jnp.exp(scores - row_max)
    denominator = jnp.sum(weights, axis=-1)
    rounded = weights.astype(jnp.bfloat16)
    mixed = jnp.einsum("hqk,khd->qhd", rounded, value_rows, preferred_element_type=jnp.float32)
    return (mixed / jnp.transpose(denominator)[:, :, None]).astype(jnp.bfloat16)


def body(queries, keys_values, key_blocks, pair_count):
    tok_dev, feature_width = queries.shape
    per_device = tok_dev // BLK
    cycle_size = lax.axis_size("blk")
    cycle_index = lax.axis_index("blk")
    lower_list = []
    upper_list = []
    lower_piece = keys_values
    upper_piece = keys_values
    for offset in range(REACH):
        lower_piece = passed_along(lower_piece, "blk", 1)
        upper_piece = passed_along(upper_piece, "blk", -1)
        lower_list.insert(0, lower_piece)
        upper_list.append(upper_piece)
    window = jnp.concatenate(lower_list + [keys_values] + upper_list, axis=1)
    window_blocks = window.shape[1] // BLK
    start_block = (cycle_index - REACH) * per_device
    positions = jnp.mod(key_blocks - start_block, cycle_size * per_device)
    query_blocks = queries.reshape(per_device, BLK, H, HD)
    key_rows = window[0].reshape(window_blocks * BLK, H, HD)
    value_rows = window[1].reshape(window_blocks * BLK, H, HD)

    def dense_block(args):
        qblock, slot_ids, live_count = args
        slot_live = jnp.arange(NB) < live_count
        block_hit = (slot_ids[:, None] == jnp.arange(window_blocks)[None, :]) & slot_live[:, None]
        live_mask = jnp.repeat(jnp.any(block_hit, axis=0), BLK)
        return attend(qblock, key_rows, value_rows, live_mask)

    result = lax.map(dense_block, (query_blocks, positions, pair_count))
    return result.reshape(tok_dev, feature_width)


def solution(mesh):
    placed = (
        P(("groups", "blk"), None),
        P(None, ("groups", "blk"), None),
        P(("groups", "blk"), None),
        P(("groups", "blk")),
    )
    return jax.shard_map(
        body, mesh=mesh, in_specs=placed, out_specs=P(("groups", "blk"), None), check_vma=False
    )
```

profile of v0, /device:TPU:1, one launch (start us, length us, event | category | flops | bytes accessed | tf_op | source)
XLA Modules:
  0.0 393.7 jit_solution(11157595790299840148)
XLA Ops:
  0.0 6.7 %copy.13 = bf16[2,384,3072]{1,2,0:T(8,128)(2,1)} copy(bf16[2,384,3072]{2,1,0:T(8,128)(2,1)} %param.7) | data formatting | bytes 9437184 | tf_op args[1]
  6.7 2.6 collective-permute-start
  9.3 0.0 collective-permute-start.2
  9.3 101.9 %collective-permute-done = bf16[2,384,3072]{1,2,0:T(8,128)(2,1)} collective-permute-done((bf16[2,384,3072]{1,2,0:T(8,128)(2,1)}, bf16[2,384,3072]{1,2,0:T(8,128)(2,1)}, u32[]{:S(2)}, u32[]{:S(2)}) %collective-permute-start) | collective-permute-done | bytes 4718624 | tf_op jit(solution)/shard_map/ppermute | solution.py:16
  111.2 2.5 collective-permute-start.1
  113.7 50.6 %collective-permute-done.2 = bf16[2,384,3072]{1,2,0:T(8,128)(2,1)} collective-permute-done((bf16[2,384,3072]{1,2,0:T(8,128)(2,1)}, bf16[2,384,3072]{1,2,0:T(8,128)(2,1)}, u32[]{:S(2)}, u32[]{:S(2)}) %collective-permute-start.2) | collective-permute-done | bytes 4718624 | tf_op jit(solution)/shard_map/ppermute | solution.py:16
  164.3 0.0 collective-permute-start.3
  164.3 3.7 copy.23
  168.0 46.9 %collective-permute-done.1 = bf16[2,384,3072]{1,2,0:T(8,128)(2,1)} collective-permute-done((bf16[2,384,3072]{1,2,0:T(8,128)(2,1)}, bf16[2,384,3072]{1,2,0:T(8,128)(2,1)}, u32[]{:S(2)}, u32[]{:S(2)}) %collective-permute-start.1) | collective-permute-done | bytes 4718624 | tf_op jit(solution)/shard_map/ppermute | solution.py:16
  214.9 2.8 constant_dynamic-update-slice_fusion.4
  217.7 3.3 constant_dynamic-update-slice_fusion.3
  221.0 0.9 constant_dynamic-update-slice_fusion.2
  222.0 3.3 constant_dynamic-update-slice_fusion.1
  225.3 0.0 collective-permute-done.3
  225.3 3.3 constant_dynamic-update-slice_fusion
  228.5 8.5 %fusion.21 = (bf16[1,1920,3072]{1,2,0:T(8,128)(2,1)}, bf16[1,1920,3072]{1,2,0:T(8,128)(2,1)}) fusion(bf16[2,1920,3072]{1,2,0:T(8,128)(2,1)S(1)} %constant_dynamic-update-slice_fusion), kind=kLoop, calls=%fused_computation.34 | loop fusion | bytes 47185920 | tf_op jit(solution)/shard_map/slice | solution.py:52
  237.1 16.3 %copy.17 = bf16[1920,24,128]{2,0,1:T(8,128)(2,1)} copy(bf16[1920,24,128]{0,2,1:T(8,128)(2,1)} %bitcast.50) | data formatting | bytes 23592960 | tf_op jit(solution)/shard_map/while | solution.py:61
  253.4 16.4 %copy.18 = bf16[1920,24,128]{2,0,1:T(8,128)(2,1)} copy(bf16[1920,24,128]{0,2,1:T(8,128)(2,1)} %bitcast.49) | data formatting | bytes 23592960 | tf_op jit(solution)/shard_map/while | solution.py:61
  269.8 0.0 copy-done.2
  269.8 121.9 %while.10 = (s32[]{:T(128)}, bf16[3,128,24,128]{3,2,1,0:T(8,128)(2,1)S(1)}, s32[3,8]{1,0:T(4,128)S(1)}, s32[3]{0:T(128)S(1)}, bf16[3,128,24,128]{3,2,1,0:T(8,128...) while((s32[]{:T(128)}, bf16[3,128,24,128]{3,2,1,0:T(8,128)(2,1)S(1)}, ...), condition=%wide.region_4.5_spmd, body=%wide.region_0.4_spmd.sunk | while | flops 3085560320 | bytes 99159800 | solution.py:61
  269.8 0.6 dynamic_slice.21
  270.4 0.6 iota_compare_fusion.3
  271.1 0.1 fusion.36
  271.2 0.1 broadcast_bitcast_fusion.2
  271.2 1.2 constant_dynamic-slice_fusion.3
  272.4 12.5 %fusion.37 = (f32[24,128]{1,0:T(8,128)S(1)}, f32[24,128,1920]{2,1,0:T(8,128)}) fusion(pred[1920]{0:T(1024)(128)(4,1)S(1)} %broadcast_bitcast_fusion.2, bf16[1920,24,128]{2,0,1:T(8,128)(2,1)} %get-tuple-element.143, bf16[1,128,24,128]{3,2,1,0:T(8,128)(2,1)S(1)} %constant_dynamic-slice_fusion.3), kind=kOutput, calls=%fused_computation.2.clone.1 | convolution fusion | flops 1527641088 | bytes 36190080 | tf_op jit(solution)/shard_map/while/body/eval_jaxpr/qhd,khd->hqk/dot_general | solution.py:20
  284.9 10.7 %fusion.38 = f32[24,128]{1,0:T(8,128)S(1)} fusion(f32[24,128,1920]{2,1,0:T(8,128)} %get-tuple-element.120, f32[24,128]{1,0:T(8,128)S(1)} %get-tuple-element.121, pred[1920]{0:T(1024)(128)(4,1)S(1)} %broadcast_bitcast_fusion.2), kind=kLoop, calls=%fused_computation.3.clone.1 | loop fusion | flops 23589888 | bytes 23619456 | tf_op jit(solution)/shard_map/while/body/eval_jaxpr/reduce_sum | solution.py:26
  295.6 14.3 %fusion.39 = bf16[1,128,24,128]{3,1,2,0:T(8,128)(2,1)S(1)} fusion(bf16[1920,24,128]{2,0,1:T(8,128)(2,1)} %get-tuple-element.144, f32[24,128,1920]{2,1,0:T(8,128)} %get-tuple-element.120, f32[24,128]{1,0:T(8,128)S(1)} %get-tuple-element.121, pred[1920]{0:T(1024)(128)(4,1)S(1)} %broadcast_bitcast_fusion.2, f32[128,24]{0,1:T(8,128)S(1)} %bitcast.56), kind=kOutput, calls=%fused_computation.12.clone.1 | convolution fusion | flops 1534328832 | bytes 36202368 | tf_op jit(solution)/shard_map/while/body/eval_jaxpr/hqk,khd->qhd/dot_general | solution.py:28
  309.9 0.6 copy_dynamic-update-slice_fusion.2
  310.5 0.6 dynamic_slice.21
  311.0 0.6 iota_compare_fusion.3
  311.7 0.1 fusion.36
  311.8 0.1 broadcast_bitcast_fusion.2
  311.9 1.2 constant_dynamic-slice_fusion.3
  313.1 12.5 %fusion.37 = (f32[24,128]{1,0:T(8,128)S(1)}, f32[24,128,1920]{2,1,0:T(8,128)}) fusion(pred[1920]{0:T(1024)(128)(4,1)S(1)} %broadcast_bitcast_fusion.2, bf16[1920,24,128]{2,0,1:T(8,128)(2,1)} %get-tuple-element.143, bf16[1,128,24,128]{3,2,1,0:T(8,128)(2,1)S(1)} %constant_dynamic-slice_fusion.3), kind=kOutput, calls=%fused_computation.2.clone.1 | convolution fusion | flops 1527641088 | bytes 36190080 | tf_op jit(solution)/shard_map/while/body/eval_jaxpr/qhd,khd->hqk/dot_general | solution.py:20
  325.6 10.7 %fusion.38 = f32[24,128]{1,0:T(8,128)S(1)} fusion(f32[24,128,1920]{2,1,0:T(8,128)} %get-tuple-element.120, f32[24,128]{1,0:T(8,128)S(1)} %get-tuple-element.121, pred[1920]{0:T(1024)(128)(4,1)S(1)} %broadcast_bitcast_fusion.2), kind=kLoop, calls=%fused_computation.3.clone.1 | loop fusion | flops 23589888 | bytes 23619456 | tf_op jit(solution)/shard_map/while/body/eval_jaxpr/reduce_sum | solution.py:26
  336.2 14.3 %fusion.39 = bf16[1,128,24,128]{3,1,2,0:T(8,128)(2,1)S(1)} fusion(bf16[1920,24,128]{2,0,1:T(8,128)(2,1)} %get-tuple-element.144, f32[24,128,1920]{2,1,0:T(8,128)} %get-tuple-element.120, f32[24,128]{1,0:T(8,128)S(1)} %get-tuple-element.121, pred[1920]{0:T(1024)(128)(4,1)S(1)} %broadcast_bitcast_fusion.2, f32[128,24]{0,1:T(8,128)S(1)} %bitcast.56), kind=kOutput, calls=%fused_computation.12.clone.1 | convolution fusion | flops 1534328832 | bytes 36202368 | tf_op jit(solution)/shard_map/while/body/eval_jaxpr/hqk,khd->qhd/dot_general | solution.py:28
  350.5 0.6 copy_dynamic-update-slice_fusion.2
  351.1 0.6 dynamic_slice.21
  351.7 0.6 iota_compare_fusion.3
  352.4 0.1 fusion.36
  352.4 0.1 broadcast_bitcast_fusion.2
  352.5 1.2 constant_dynamic-slice_fusion.3
  353.7 12.5 %fusion.37 = (f32[24,128]{1,0:T(8,128)S(1)}, f32[24,128,1920]{2,1,0:T(8,128)}) fusion(pred[1920]{0:T(1024)(128)(4,1)S(1)} %broadcast_bitcast_fusion.2, bf16[1920,24,128]{2,0,1:T(8,128)(2,1)} %get-tuple-element.143, bf16[1,128,24,128]{3,2,1,0:T(8,128)(2,1)S(1)} %constant_dynamic-slice_fusion.3), kind=kOutput, calls=%fused_computation.2.clone.1 | convolution fusion | flops 1527641088 | bytes 36190080 | tf_op jit(solution)/shard_map/while/body/eval_jaxpr/qhd,khd->hqk/dot_general | solution.py:20
  366.2 10.7 %fusion.38 = f32[24,128]{1,0:T(8,128)S(1)} fusion(f32[24,128,1920]{2,1,0:T(8,128)} %get-tuple-element.120, f32[24,128]{1,0:T(8,128)S(1)} %get-tuple-element.121, pred[1920]{0:T(1024)(128)(4,1)S(1)} %broadcast_bitcast_fusion.2), kind=kLoop, calls=%fused_computation.3.clone.1 | loop fusion | flops 23589888 | bytes 23619456 | tf_op jit(solution)/shard_map/while/body/eval_jaxpr/reduce_sum | solution.py:26
  376.9 14.3 %fusion.39 = bf16[1,128,24,128]{3,1,2,0:T(8,128)(2,1)S(1)} fusion(bf16[1920,24,128]{2,0,1:T(8,128)(2,1)} %get-tuple-element.144, f32[24,128,1920]{2,1,0:T(8,128)} %get-tuple-element.120, f32[24,128]{1,0:T(8,128)S(1)} %get-tuple-element.121, pred[1920]{0:T(1024)(128)(4,1)S(1)} %broadcast_bitcast_fusion.2, f32[128,24]{0,1:T(8,128)S(1)} %bitcast.56), kind=kOutput, calls=%fused_computation.12.clone.1 | convolution fusion | flops 1534328832 | bytes 36202368 | tf_op jit(solution)/shard_map/while/body/eval_jaxpr/hqk,khd->qhd/dot_general | solution.py:28
  391.1 0.6 copy_dynamic-update-slice_fusion.2
  391.7 2.0 copy.31
  (15 shorter events, 0.1 us)
Async XLA Ops:
  0.0 168.0 %copy-start.1 = (s32[3,8]{1,0:T(4,128)S(1)}, s32[3,8]{1,0:T(4,128)}, u32[]{:S(2)}) copy-start(s32[3,8]{1,0:T(4,128)} %param.8) | copy-start | bytes 292
  6.7 104.6 %collective-permute-start = (bf16[2,384,3072]{1,2,0:T(8,128)(2,1)}, bf16[2,384,3072]{1,2,0:T(8,128)(2,1)}, u32[]{:S(2)}, u32[]{:S(2)}) collective-permute-start(bf16[2,384,3072]{1,2,0:T(8,128)(2,1)} %copy.13), channel_id=1, source_target_pairs={{0,1},{1,2},{2,3},{3,4},{4,5},{5,6},{6,7},{7,8},{8,9},{9,10},{10,1... | collective-permute-start | bytes 14155784 | tf_op jit(solution)/shard_map/ppermute | solution.py:16
  9.3 155.0 %collective-permute-start.2 = (bf16[2,384,3072]{1,2,0:T(8,128)(2,1)}, bf16[2,384,3072]{1,2,0:T(8,128)(2,1)}, u32[]{:S(2)}, u32[]{:S(2)}) collective-permute-start(bf16[2,384,3072]{1,2,0:T(8,128)(2,1)} %copy.13), channel_id=1, source_target_pairs={{0,15},{1,0},{2,1},{3,2},{4,3},{5,4},{6,5},{7,6},{8,7},{9,8},{10,9... | collective-permute-start | bytes 14155784 | tf_op jit(solution)/shard_map/ppermute | solution.py:16
  111.2 103.7 %collective-permute-start.1 = (bf16[2,384,3072]{1,2,0:T(8,128)(2,1)}, bf16[2,384,3072]{1,2,0:T(8,128)(2,1)}, u32[]{:S(2)}, u32[]{:S(2)}) collective-permute-start(bf16[2,384,3072]{1,2,0:T(8,128)(2,1)} %collective-permute-done), channel_id=1, source_target_pairs={{0,1},{1,2},{2,3},{3,4},{4,5},{5,6},{6,7},{7,8},{8,9},{9,10},{10,1... | collective-permute-start | bytes 14155784 | tf_op jit(solution)/shard_map/ppermute | solution.py:16
  164.3 61.0 %collective-permute-start.3 = (bf16[2,384,3072]{1,2,0:T(8,128)(2,1)}, bf16[2,384,3072]{1,2,0:T(8,128)(2,1)}, u32[]{:S(2)}, u32[]{:S(2)}) collective-permute-start(bf16[2,384,3072]{1,2,0:T(8,128)(2,1)} %collective-permute-done.2), channel_id=1, source_target_pairs={{0,15},{1,0},{2,1},{3,2},{4,3},{5,4},{6,5},{7,6},{8,7},{9,8},{10,9... | collective-permute-start | bytes 14155784 | tf_op jit(solution)/shard_map/ppermute | solution.py:16
  164.3 56.7 %slice-start = ((s8[4718592]{0:T(1024)(128)(4,1)}), s8[524288]{0:T(1024)(128)(4,1)S(1)}, s32[]{:S(2)}) async-start(s8[4718592]{0:T(1024)(128)(4,1)} %bitcast.51), calls=%async_computation | async-start | bytes 1048576
  168.0 53.0 %slice-start.1 = ((s8[4718592]{0:T(1024)(128)(4,1)}), s8[4194304]{0:T(1024)(128)(4,1)S(1)}, s32[]{:S(2)}) async-start(s8[4718592]{0:T(1024)(128)(4,1)} %bitcast.51), calls=%async_computation.1 | async-start | bytes 8388608
  253.4 16.4 %copy-start = (bf16[3,128,24,128]{3,2,1,0:T(8,128)(2,1)S(1)}, bf16[3,128,24,128]{3,2,1,0:T(8,128)(2,1)}, u32[]{:S(2)}) copy-start(bf16[3,128,24,128]{3,2,1,0:T(8,128)(2,1)} %custom-call.1) | copy-start | bytes 7077892
  253.4 16.4 %copy-start.2 = (s32[3]{0:T(128)S(1)}, s32[3]{0:T(128)}, u32[]{:S(2)}) copy-start(s32[3]{0:T(128)} %param.9) | copy-start | bytes 40
where the time goes:
time: 395 us; the launch traced here: 394 us
  waiting for transfers between devices  199 us (50%)
  matrix products  80.2 us (20%)
  local copies, waits for them, and re-layouts  74.6 us (19%)
  other arithmetic  34.2 us (9%)
  starting transfers between devices  5.11 us (1%)
    ppermute x4, waiting for transfers between devices, passed_along(): return lax.ppermute(value, axis, pairs)  199 us
    dot_general x3, matrix products, attend(): jnp.einsum('hqk,khd->qhd', rounded, value_rows, preferred_element_type=jn...  42.8 us
    dot_general x3, matrix products, attend(): jnp.einsum('qhd,khd->hqk', qblock, key_rows, preferred_element_type=jnp.f...  37.4 us
    while x2, local copies, waits for them, and re-layouts, body(): result = lax.map(dense_block, (query_blocks, positions, pair_count))  32.7 us
    reduce_sum x3, other arithmetic, attend(): denominator = jnp.sum(weights, axis=-1)  32 us
    unnamed x17, local copies, waits for them, and re-layouts  22.7 us
    slice x1, local copies, waits for them, and re-layouts, body(): value_rows = window[1].reshape(window_blocks * BLK, H, HD)  8.53 us
  transfers between devices with their start and end apart: 4, of which 3 were waited for; matrix products, arithmetic and copies ran while one was open for 4% of the time, Pallas kernels for 0%

commit v1 on v0

v1 whole, which is shorter than its diff:
```python
import functools

import jax
import jax.numpy as jnp
from jax import lax
from jax.experimental import pallas as pl
from jax.experimental.pallas import tpu as pltpu
from jax.sharding import PartitionSpec as P

HD = 128
BLK = 128
NB = 8
AHEAD = 3
MESH = pl.DeviceIdType.MESH
FAR = -1e30
SCALE = HD ** (-0.5) * 1.4426950408889634


def kernel(n, q_hbm, kv_hbm, blocks_ref, count_ref, out_hbm,
           q_v, own_v, held, out_v, bias,
           in_sem, out_sem,
           y_send, c_send, z_send, p_send, recv):
    groups = held.shape[1]
    rows = q_v.shape[0]
    per_device = rows // BLK
    me = lax.axis_index("blk")
    core = me % 2
    side = (me // 2) % 2
    y_dev = me + 2 - 4 * side
    c_dev = me + 1 - 2 * core
    up = lax.rem(me + 4, n)
    down = lax.rem(me + n - 4, n)
    z_dev = jnp.where(side == 0, up, down)
    far_step = n - 2 + 4 * side
    passed_slot = (side + core) % 2
    other_passes_far = 1 - passed_slot
    far_dev = lax.rem(me + far_step, n)
    pass_dev = jnp.where(
        other_passes_far == 1,
        lax.rem(c_dev + far_step, n),
        c_dev + 2 - 4 * side,
    )
    sources = [me, y_dev, far_dev, c_dev, pass_dev]

    def columns(g):
        return pl.ds(pl.multiple_of(g * HD, HD), HD)

    def y_copy(g):
        return pltpu.make_async_remote_copy(
            src_ref=kv_hbm.at[:, :, columns(g)], dst_ref=held.at[0, g],
            send_sem=y_send.at[g], recv_sem=recv.at[0, g],
            device_id={"blk": y_dev}, device_id_type=MESH)

    def z_copy(g):
        return pltpu.make_async_remote_copy(
            src_ref=held.at[0, g], dst_ref=held.at[1, g],
            send_sem=z_send.at[g], recv_sem=recv.at[1, g],
            device_id={"blk": z_dev}, device_id_type=MESH)

    def c_copy(g):
        return pltpu.make_async_remote_copy(
            src_ref=kv_hbm.at[:, :, columns(g)], dst_ref=held.at[2, g],
            send_sem=c_send.at[g], recv_sem=recv.at[2, g],
            device_id={"blk": c_dev}, device_id_type=MESH)

    def p_copy(g):
        return pltpu.make_async_remote_copy(
            src_ref=held.at[passed_slot, g], dst_ref=held.at[3, g],
            send_sem=p_send.at[g], recv_sem=recv.at[3, g],
            device_id={"blk": c_dev}, device_id_type=MESH)

    def out_copy(g):
        return pltpu.make_async_copy(
            out_v.at[:, columns(g)], out_hbm.at[:, columns(g)], out_sem.at[g])

    q_in = pltpu.make_async_copy(q_hbm, q_v, in_sem.at[0])
    own_in = pltpu.make_async_copy(kv_hbm, own_v, in_sem.at[1])

    barrier = pltpu.get_barrier_semaphore()
    for dev in (y_dev, c_dev, up, down):
        pl.semaphore_signal(barrier, inc=1, device_id={"blk": dev}, device_id_type=MESH)
    pl.semaphore_wait(barrier, 4)

    for g in range(min(AHEAD, groups)):
        y_copy(g).start()
        c_copy(g).start()
    q_in.start()
    own_in.start()

    for r in range(per_device):
        for s, dev in enumerate(sources):
            for j in range(per_device):
                block = dev * per_device + j
                hit = jnp.int32(0)
                for i in range(NB):
                    listed = (blocks_ref[r, i] == block) & (i < count_ref[r])
                    hit = jnp.where(listed, 1, hit)
                value = jnp.where(hit == 1, 0.0, FAR).astype(jnp.float32)
                at = s * rows + j * BLK
                bias[r, :, at:at + BLK] = jnp.full((8, BLK), value, jnp.float32)
    q_in.wait()
    own_in.wait()

    def attend(g):
        q = q_v[:, columns(g)]
        keys = [own_v[0, :, columns(g)]] + [held[s, g, 0] for s in range(4)]
        values = [own_v[1, :, columns(g)]] + [held[s, g, 1] for s in range(4)]
        top = None
        scores = []
        for s in range(5):
            part = lax.dot_general(
                q, keys[s], (((1,), (1,)), ((), ())),
                preferred_element_type=jnp.float32)
            part = jnp.concatenate(
                [part[r * BLK:(r + 1) * BLK] + bias[r, 0:1, s * rows:(s + 1) * rows]
                 for r in range(per_device)], axis=0)
            best = jnp.max(part, axis=-1, keepdims=True)
            top = best if top is None else jnp.maximum(top, best)
            scores.append(part)
        total = None
        mixed = None
        for s in range(5):
            weights = jnp.exp2((scores[s] - top) * SCALE)
            added = jnp.sum(weights, axis=-1, keepdims=True)
            product = jnp.dot(
                weights.astype(jnp.bfloat16), values[s],
                preferred_element_type=jnp.float32)
            total = added if total is None else total + added
            mixed = product if mixed is None else mixed + product
        out_v[:, columns(g)] = (mixed / total).astype(out_v.dtype)

    def step(t, carry):
        @pl.when(t < groups)
        def _():
            y_copy(t).wait_recv()
            z_copy(t).start()
            y_copy(t).wait_send()
            c_copy(t).wait_send()

            @pl.when(t + AHEAD < groups)
            def _():
                y_copy(t + AHEAD).start()
                c_copy(t + AHEAD).start()

        @pl.when((t >= 1) & (t < groups + 1))
        def _():
            z_copy(t - 1).wait_recv()
            p_copy(t - 1).start()

        @pl.when(t >= 2)
        def _():
            g = t - 2
            c_copy(g).wait_recv()
            p_copy(g).wait_recv()
            attend(g)
            out_copy(g).start()

        return carry

    lax.fori_loop(0, groups + 2, step, 0)

    def finish(g, carry):
        z_copy(g).wait_send()
        p_copy(g).wait_send()
        out_copy(g).wait()
        return carry

    lax.fori_loop(0, groups, finish, 0)


def body(queries, keys_values, key_blocks, pair_count):
    rows, width = queries.shape
    groups = width // HD
    per_device = rows // BLK
    n = lax.axis_size("blk")
    any_spec = pl.BlockSpec(memory_space=pl.ANY)
    smem_spec = pl.BlockSpec(memory_space=pltpu.SMEM)
    dma = pltpu.SemaphoreType.DMA
    return pl.pallas_call(
        functools.partial(kernel, n),
        out_shape=jax.ShapeDtypeStruct((rows, width), jnp.bfloat16),
        in_specs=[any_spec, any_spec, smem_spec, smem_spec],
        out_specs=any_spec,
        scratch_shapes=[
            pltpu.VMEM((rows, width), jnp.bfloat16),
            pltpu.VMEM((2, rows, width), jnp.bfloat16),
            pltpu.VMEM((4, groups, 2, rows, HD), jnp.bfloat16),
            pltpu.VMEM((rows, width), jnp.bfloat16),
            pltpu.VMEM((per_device, 8, 5 * rows), jnp.float32),
            dma((2,)),
            dma((groups,)),
            dma((groups,)),
            dma((groups,)),
            dma((groups,)),
            dma((groups,)),
            dma((4, groups)),
        ],
        compiler_params=pltpu.CompilerParams(
            collective_id=0, has_side_effects=True,
            vmem_limit_bytes=56 * 1024 * 1024),
        cost_estimate=pl.CostEstimate(
            flops=4 * rows * 5 * rows * width,
            bytes_accessed=16 * rows * width,
            transcendentals=groups * rows * 5 * rows),
    )(queries, keys_values, key_blocks, pair_count)


def solution(mesh):
    placed = (
        P(("groups", "blk"), None),
        P(None, ("groups", "blk"), None),
        P(("groups", "blk"), None),
        P(("groups", "blk")),
    )
    return jax.shard_map(
        body, mesh=mesh, in_specs=placed, out_specs=P(("groups", "blk"), None), check_vma=False
    )
```

time: 395 us -> 123 us (0.31)
  waiting for transfers between devices: 199 us -> 0 us
  Pallas kernels: 0 us -> 119 us
  matrix products: 80.2 us -> 0 us
  local copies, waits for them, and re-layouts: 74.6 us -> 3.22 us
  other arithmetic: 34.2 us -> 0 us
  starting transfers between devices: 5.11 us -> 0 us
    ppermute x4 -> x0, waiting for transfers between devices: 199 us -> none  [passed_along(): return lax.ppermute(value, axis, pairs)]
    pallas_call x0 -> x1, Pallas kernels: none -> 119 us  [body(): pl.pallas_call(functools.partial(kernel, n), out_shape=jax.ShapeDtypeStru...]
    dot_general x6 -> x0, matrix products: 80.2 us -> none  [the longest x3 42.8 us: attend(): jnp.einsum('hqk,khd->qhd', rounded, value_rows, preferred_element_type=jn...]
    while x2 -> x0, local copies, waits for them, and re-layouts: 32.7 us -> none  [body(): result = lax.map(dense_block, (query_blocks, positions, pair_count))]
    reduce_sum x3 -> x0, other arithmetic: 32 us -> none  [attend(): denominator = jnp.sum(weights, axis=-1)]
    unnamed x17 -> x1, local copies, waits for them, and re-layouts: 22.7 us -> 3.22 us
    slice x1 -> x0, local copies, waits for them, and re-layouts: 8.53 us -> none  [body(): value_rows = window[1].reshape(window_blocks * BLK, H, HD)]
    dynamic_slice x6 -> x0, local copies, waits for them, and re-layouts: 5.4 us -> none  [body(): result = lax.map(dense_block, (query_blocks, positions, pair_count))]
  transfers between devices with their start and end apart: 4 -> 0, of which waited for: 3 -> 0; matrix products, arithmetic and copies ran while one was open for 4% -> 0% of each run, Pallas kernels for 0% -> 0%
where the time goes in v1:
time: 123 us
  Pallas kernels  119 us (97%)
  local copies, waits for them, and re-layouts  3.22 us (3%)
    pallas_call x1, Pallas kernels, body(): pl.pallas_call(functools.partial(kernel, n), out_shape=jax.ShapeDtypeStru...  119 us
    unnamed x1, local copies, waits for them, and re-layouts  3.22 us

profile of v1, /device:TPU:1, one launch (start us, length us, event | category | flops | bytes accessed | tf_op | source)
XLA Modules:
  0.0 122.7 jit_solution(4216769512012079027)
XLA Ops:
  0.0 119.5 %shard_map.46 = bf16[384,3072]{1,0:T(8,128)(2,1)} custom-call(bf16[384,3072]{1,0:T(8,128)(2,1)} %q_hbm.1, bf16[2,384,3072]{2,1,0:T(8,128)(2,1)} %kv_hbm.1, s32[3,8]{1,0:T(4,128)} %blocks_ref.1, s32[3]{0:T(128)} %count_ref.1), custom_call_target="tpu_custom_call" | custom-call | flops 9059696640 | bytes 18874368 | tf_op jit(solution)/shard_map/pallas_call | solution.py:179
  119.5 3.2 %copy.6 = bf16[384,3072]{1,0:T(8,128)(2,1)} copy(bf16[384,3072]{1,0:T(8,128)(2,1)} %shard_map.46) | data formatting | bytes 4718592

commit v2 on v1

v2 whole, which is shorter than its diff:
```python
import functools

import jax
import jax.numpy as jnp
from jax import lax
from jax.experimental import pallas as pl
from jax.experimental.pallas import tpu as pltpu
from jax.sharding import PartitionSpec as P

HD = 128
BLK = 128
NB = 8
SPLIT = 1
Z_LAG = 2
P_LAG = 1
AHEAD = 6
MESH = pl.DeviceIdType.MESH
FAR = -1e30
SCALE = HD ** (-0.5) * 1.4426950408889634


def kernel(n, q_hbm, kv_hbm, blocks_ref, count_ref, out_v,
           q_v, own_v, mate_v, held, bias, weights_v, total_v,
           in_sem, c_sem, y_send, z_send, p_send, recv):
    rows, width = q_v.shape
    groups = width // HD
    parts = 2 * SPLIT
    part_rows = rows // SPLIT
    pieces = groups * parts
    per_device = rows // BLK
    me = lax.axis_index("blk")
    core = me % 2
    side = (me // 2) % 2
    y_dev = me + 2 - 4 * side
    c_dev = me + 1 - 2 * core
    up = lax.rem(me + 4, n)
    down = lax.rem(me + n - 4, n)
    z_dev = jnp.where(side == 0, up, down)
    far_step = n - 2 + 4 * side
    passed_slot = (side + core) % 2
    other_passes_far = 1 - passed_slot
    far_dev = lax.rem(me + far_step, n)
    pass_dev = jnp.where(
        other_passes_far == 1,
        lax.rem(c_dev + far_step, n),
        c_dev + 2 - 4 * side,
    )
    sources = [me, y_dev, far_dev, pass_dev, c_dev]

    def columns(g):
        return pl.ds(pl.multiple_of(g * HD, HD), HD)

    def piece(p):
        g, k = p // parts, p % parts
        at = pl.multiple_of(k % SPLIT * part_rows, part_rows)
        return kv_hbm.at[k // SPLIT, pl.ds(at, part_rows), columns(g)]

    def landed(slot, p):
        g, k = p // parts, p % parts
        at = pl.multiple_of(k % SPLIT * part_rows, part_rows)
        return held.at[slot, g, k // SPLIT, pl.ds(at, part_rows)]

    def y_copy(g):
        return pltpu.make_async_remote_copy(
            src_ref=piece(g), dst_ref=landed(0, g),
            send_sem=y_send.at[g], recv_sem=recv.at[0, g],
            device_id={"blk": y_dev}, device_id_type=MESH)

    def z_copy(g):
        return pltpu.make_async_remote_copy(
            src_ref=landed(0, g), dst_ref=landed(1, g),
            send_sem=z_send.at[g], recv_sem=recv.at[1, g],
            device_id={"blk": z_dev}, device_id_type=MESH)

    c_copy = pltpu.make_async_remote_copy(
        src_ref=kv_hbm, dst_ref=mate_v,
        send_sem=c_sem.at[0], recv_sem=c_sem.at[1],
        device_id={"blk": c_dev}, device_id_type=MESH)

    def p_copy(g):
        return pltpu.make_async_remote_copy(
            src_ref=landed(passed_slot, g), dst_ref=landed(2, g),
            send_sem=p_send.at[g], recv_sem=recv.at[2, g],
            device_id={"blk": c_dev}, device_id_type=MESH)

    q_in = pltpu.make_async_copy(q_hbm, q_v, in_sem.at[0])
    own_in = pltpu.make_async_copy(kv_hbm, own_v, in_sem.at[1])

    barrier = pltpu.get_barrier_semaphore()
    for dev in (y_dev, c_dev, up, down):
        pl.semaphore_signal(barrier, inc=1, device_id={"blk": dev}, device_id_type=MESH)
    pl.semaphore_wait(barrier, 4)

    for g in range(min(AHEAD, pieces)):
        y_copy(g).start()
    q_in.start()
    own_in.start()
    c_copy.start()

    for r in range(per_device):
        for s, dev in enumerate(sources):
            for j in range(per_device):
                block = dev * per_device + j
                hit = jnp.int32(0)
                for i in range(NB):
                    listed = (blocks_ref[r, i] == block) & (i < count_ref[r])
                    hit = jnp.where(listed, 1, hit)
                value = jnp.where(hit == 1, 0.0, FAR).astype(jnp.float32)
                at = s * rows + j * BLK
                bias[r, :, at:at + BLK] = jnp.full((8, BLK), value, jnp.float32)
    q_in.wait()
    own_in.wait()

    def weigh(g):
        q = q_v[:, columns(g)]
        keys = [own_v[0, :, columns(g)]]
        keys += [held[s, g, 0] for s in range(3)]
        keys += [mate_v[0, :, columns(g)]]
        top = None
        scores = []
        for s in range(5):
            part = lax.dot_general(
                q, keys[s], (((1,), (1,)), ((), ())),
                preferred_element_type=jnp.float32)
            part = jnp.concatenate(
                [part[r * BLK:(r + 1) * BLK] + bias[r, 0:1, s * rows:(s + 1) * rows]
                 for r in range(per_device)], axis=0)
            best = jnp.max(part, axis=-1, keepdims=True)
            top = best if top is None else jnp.maximum(top, best)
            scores.append(part)
        total = None
        for s in range(5):
            weights = jnp.exp2((scores[s] - top) * SCALE)
            added = jnp.sum(weights, axis=-1, keepdims=True)
            total = added if total is None else total + added
            weights_v[s] = weights.astype(jnp.bfloat16)
        total_v[...] = jnp.broadcast_to(1.0 / total, total_v.shape)

    def mix(g):
        values = [own_v[1, :, columns(g)]]
        values += [held[s, g, 1] for s in range(3)]
        values += [mate_v[1, :, columns(g)]]
        mixed = None
        for s in range(5):
            product = jnp.dot(
                weights_v[s], values[s], preferred_element_type=jnp.float32)
            mixed = product if mixed is None else mixed + product
        out_v[:, columns(g)] = (mixed * total_v[...]).astype(out_v.dtype)

    def step(t, carry):
        @pl.when(t < pieces)
        def _():
            y_copy(t).wait_recv()
            z_copy(t).start()
            y_copy(t).wait_send()

            @pl.when(t + AHEAD < pieces)
            def _():
                y_copy(t + AHEAD).start()

        @pl.when((t >= Z_LAG) & (t < pieces + Z_LAG))
        def _():
            z_copy(t - Z_LAG).wait_recv()
            p_copy(t - Z_LAG).start()

        done = t - Z_LAG - P_LAG

        @pl.when(done == 0)
        def _():
            c_copy.wait_recv()

        @pl.when(done >= 0)
        def _():
            p_copy(done).wait_recv()

        @pl.when((done >= 0) & (done % parts == SPLIT - 1))
        def _():
            weigh(done // parts)

        @pl.when((done >= 0) & (done % parts == parts - 1))
        def _():
            mix(done // parts)

        return carry

    lax.fori_loop(0, pieces + Z_LAG + P_LAG, step, 0)

    def finish(p, carry):
        z_copy(p).wait_send()
        p_copy(p).wait_send()
        return carry

    lax.fori_loop(0, pieces, finish, 0)
    c_copy.wait_send()


def body(queries, keys_values, key_blocks, pair_count):
    rows, width = queries.shape
    groups = width // HD
    pieces = 2 * SPLIT * groups
    per_device = rows // BLK
    n = lax.axis_size("blk")
    any_spec = pl.BlockSpec(memory_space=pl.ANY)
    smem_spec = pl.BlockSpec(memory_space=pltpu.SMEM)
    dma = pltpu.SemaphoreType.DMA
    return pl.pallas_call(
        functools.partial(kernel, n),
        out_shape=pltpu.VMEM((rows, width), jnp.bfloat16),
        in_specs=[any_spec, any_spec, smem_spec, smem_spec],
        out_specs=pl.BlockSpec(memory_space=pltpu.VMEM),
        scratch_shapes=[
            pltpu.VMEM((rows, width), jnp.bfloat16),
            pltpu.VMEM((2, rows, width), jnp.bfloat16),
            pltpu.VMEM((2, rows, width), jnp.bfloat16),
            pltpu.VMEM((3, groups, 2, rows, HD), jnp.bfloat16),
            pltpu.VMEM((per_device, 8, 5 * rows), jnp.float32),
            pltpu.VMEM((5, rows, rows), jnp.bfloat16),
            pltpu.VMEM((rows, HD), jnp.float32),
            dma((2,)),
            dma((2,)),
            dma((pieces,)),
            dma((pieces,)),
            dma((pieces,)),
            dma((3, pieces)),
        ],
        compiler_params=pltpu.CompilerParams(
            collective_id=0, has_side_effects=True,
            vmem_limit_bytes=56 * 1024 * 1024),
        cost_estimate=pl.CostEstimate(
            flops=4 * rows * 5 * rows * width,
            bytes_accessed=16 * rows * width,
            transcendentals=groups * rows * 5 * rows),
    )(queries, keys_values, key_blocks, pair_count)


def solution(mesh):
    placed = (
        P(("groups", "blk"), None),
        P(None, ("groups", "blk"), None),
        P(("groups", "blk"), None),
        P(("groups", "blk")),
    )
    return jax.shard_map(
        body, mesh=mesh, in_specs=placed, out_specs=P(("groups", "blk"), None), check_vma=False
    )
```

time: 123 us -> 120 us (0.976)
  local copies, waits for them, and re-layouts: 3.22 us -> 1.41 us
    pallas_call x1, Pallas kernels: 119 us -> 118 us  [body(): pl.pallas_call(functools.partial(kernel, n), out_shape=pltpu.VMEM((rows,...]
    unnamed x1, local copies, waits for them, and re-layouts: 3.22 us -> 1.41 us
where the time goes in v2:
time: 120 us; the launch traced here: 119 us
  Pallas kernels  118 us (98%)
  local copies, waits for them, and re-layouts  1.41 us (1%)
    pallas_call x1, Pallas kernels, body(): pl.pallas_call(functools.partial(kernel, n), out_shape=pltpu.VMEM((rows,...  118 us

profile of v2, /device:TPU:1, one launch (start us, length us, event | category | flops | bytes accessed | tf_op | source)
XLA Modules:
  0.0 119.1 jit_solution(10284022781334179250)
XLA Ops:
  0.0 117.7 %shard_map.46 = bf16[384,3072]{1,0:T(8,128)(2,1)S(1)} custom-call(bf16[384,3072]{1,0:T(8,128)(2,1)} %q_hbm.1, bf16[2,384,3072]{2,1,0:T(8,128)(2,1)} %kv_hbm.1, s32[3,8]{1,0:T(4,128)} %blocks_ref.1, s32[3]{0:T(128)} %count_ref.1), custom_call_target="tpu_custom_call" | custom-call | flops 9059696640 | bytes 18874368 | tf_op jit(solution)/shard_map/pallas_call | solution.py:206
  117.7 1.4 %copy.6 = bf16[384,3072]{1,0:T(8,128)(2,1)} copy(bf16[384,3072]{1,0:T(8,128)(2,1)S(1)} %shard_map.46) | data formatting | bytes 4718592
